TPU v7x, 32 devices: a whole 2x2x4 slice. The times are simulated.
32 devices in a mesh: dp: 4 (over x, core), sp: 8 (over z, y).
Axes of the slice: x: 2, y: 2, z: 4, core: 2. Of those that a mesh axis runs over, the one named last changes fastest.
Arguments:
- frames_in: bfloat16 [2048, 64, 256], P(('dp', 'sp')), may hold values from -6 to 6
- spatial_weight: bfloat16 [3, 3, 256, 256], replicated, may hold values from -0.125 to 0.125
- temporal_weight: bfloat16 [3, 256, 256], replicated, may hold values from -0.21875 to 0.21875
- cotangent: bfloat16 [2048, 64, 256], P(('dp', 'sp')), may hold values from -6 to 6
Outputs:
- block_out: bfloat16 [2048, 64, 256], P(('dp', 'sp'))
- grad_input: bfloat16 [2048, 64, 256], P(('dp', 'sp'))
- grad_spatial: float32 [3, 3, 256, 256], replicated
- grad_temporal: float32 [3, 256, 256], replicated
All inputs are finite; a program needn't handle non-finite values.
Results may differ from a plain program's by a relative error of at most 0.0049.
Values may be sent and summed in bfloat16 or wider, within the bound.
A program may use at most 128 MiB of HBM per device.

v0:
```python
import math
import jax
import jax.numpy as jnp
from jax import lax
from jax.sharding import PartitionSpec as P

H = 64
FRAMES = 4


def contract_rows(left, right):
    return lax.dot_general(
        left, right, (((0,), (0,)), ((), ())), preferred_element_type=jnp.float32
    )


def times_transpose(left, weight):
    return lax.dot_general(
        left, weight, (((1,), (1,)), ((), ())), preferred_element_type=jnp.float32
    )


def local(frames_in, spatial_weight, temporal_weight, cotangent):
    slab_rows, width_cells, channels = frames_in.shape
    sp_count = lax.axis_size("sp")

    def padded_rows(values):
        return jnp.pad(values, ((1, 1), (1, 1), (0, 0)))

    def flatten_rows(values):
        return values.reshape(-1, channels)

    padded_in = padded_rows(frames_in)
    pre = jnp.zeros((slab_rows * width_cells, channels), jnp.float32)
    for tap_row in range(3):
        for tap_col in range(3):
            window = flatten_rows(
                padded_in[tap_row : tap_row + slab_rows, tap_col : tap_col + width_cells]
            )
            pre = pre + jnp.dot(
                window, spatial_weight[tap_row, tap_col], preferred_element_type=jnp.float32
            )
    act = jax.nn.silu(pre).astype(jnp.bfloat16).reshape(slab_rows, width_cells, channels)

    def to_frames(values):
        return lax.all_to_all(values, "sp", split_axis=0, concat_axis=1, tiled=True)

    moved_act, moved_cot = (
        lax.all_to_all(act, "sp", split_axis=1, concat_axis=0, tiled=True),
        lax.all_to_all(cotangent, "sp", split_axis=1, concat_axis=0, tiled=True),
    )
    group_rows = slab_rows * sp_count
    stripe = width_cells // sp_count
    groups = group_rows // (FRAMES * H)
    act_clips = moved_act.reshape(groups, FRAMES, H * stripe, channels)
    cot_clips = moved_cot.reshape(groups, FRAMES, H * stripe, channels)
    act_padded = jnp.pad(act_clips, ((0, 0), (2, 0), (0, 0), (0, 0)))
    cot_padded = jnp.pad(cot_clips, ((0, 0), (0, 2), (0, 0), (0, 0)))
    temporal_sum = jnp.zeros(act_clips.shape, jnp.float32)
    act_grad_sum = jnp.zeros(act_clips.shape, jnp.float32)
    temporal_terms = []
    for tap_step in range(3):
        earlier = act_padded[:, 2 - tap_step : 2 - tap_step + FRAMES]
        temporal_sum = temporal_sum + jnp.einsum(
            "gfpc,cd->gfpd", earlier, temporal_weight[tap_step], preferred_element_type=jnp.float32
        )
        temporal_terms.append(
            jnp.einsum("gfpc,gfpd->cd", earlier, cot_clips, preferred_element_type=jnp.float32)
        )
        later = cot_padded[:, tap_step : tap_step + FRAMES]
        act_grad_sum = act_grad_sum + jnp.einsum(
            "gfpd,cd->gfpc", later, temporal_weight[tap_step], preferred_element_type=jnp.float32
        )
    temporal_out = to_frames(
        temporal_sum.astype(jnp.bfloat16).reshape(group_rows, stripe, channels)
    )
    grad_act = to_frames(act_grad_sum.astype(jnp.bfloat16).reshape(group_rows, stripe, channels))
    grad_temporal = jnp.stack(temporal_terms)
    grad_scale = 1.0 / math.sqrt(slab_rows * sp_count * lax.axis_size("dp") * width_cells)
    block_out = (frames_in.astype(jnp.float32) + temporal_out.astype(jnp.float32)).astype(
        jnp.bfloat16
    )
    sigma = jax.nn.sigmoid(pre)
    grad_pre = (
        flatten_rows(grad_act).astype(jnp.float32) * (sigma * (1.0 + pre * (1.0 - sigma)))
    ).astype(jnp.bfloat16)
    grad_padded = padded_rows(grad_pre.reshape(slab_rows, width_cells, channels))
    spatial_terms = []
    grad_in = flatten_rows(cotangent).astype(jnp.float32)
    for tap_row in range(3):
        for tap_col in range(3):
            window = flatten_rows(
                padded_in[tap_row : tap_row + slab_rows, tap_col : tap_col + width_cells]
            )
            spatial_terms.append(contract_rows(window, grad_pre))
            back_window = flatten_rows(
                grad_padded[
                    2 - tap_row : 2 - tap_row + slab_rows, 2 - tap_col : 2 - tap_col + width_cells
                ]
            )
            grad_in = grad_in + times_transpose(back_window, spatial_weight[tap_row, tap_col])
    grad_spatial = jnp.stack(spatial_terms).reshape(3, 3, channels, channels)
    grad_spatial, grad_temporal = lax.psum((grad_spatial, grad_temporal), ("dp", "sp"))
    grad_input = grad_in.astype(jnp.bfloat16).reshape(slab_rows, width_cells, channels)
    return (block_out, grad_input, grad_spatial * grad_scale, grad_temporal * grad_scale)


def solution(mesh):
    placed = (P(("dp", "sp"), None, None), P(), P(), P(("dp", "sp"), None, None))
    return jax.shard_map(
        local,
        mesh=mesh,
        in_specs=placed,
        out_specs=(P(("dp", "sp"), None, None), P(("dp", "sp"), None, None), P(), P()),
        check_vma=False,
    )
```

profile of v0, /device:TPU:0, one launch (start us, length us, event | category | flops | bytes accessed | tf_op | source)
XLA Modules:
  0.0 385.7 jit_solution(17746489602125472998)
XLA Ops:
  7.2 4.1 %copy.32 = bf16[64,64,256]{2,0,1:T(8,128)(2,1)} copy(bf16[64,64,256]{2,1,0:T(8,128)(2,1)} %param.7) | data formatting | bytes 4194304 | tf_op args[3]
  11.3 7.4 %all-to-all-start.2 = ((bf16[64,64,256]{2,0,1:T(8,128)(2,1)}), bf16[64,64,256]{2,0,1:T(8,128)(2,1)}, u32[]{:S(2)}, u32[]{:S(2)}) async-start(bf16[64,64,256]{2,0,1:T(8,128)(2,1)} %copy.32), calls=%async_computation.2 | async-start | bytes 4194304 | tf_op jit(solution)/shard_map/all_to_all | solution.py:50
  18.7 9.8 %pad_slice_fusion.10 = (bf16[64,64,256]{2,1,0:T(8,128)(2,1)}, bf16[64,64,256]{2,1,0:T(8,128)(2,1)}, bf16[64,64,256]{2,1,0:T(8,128)(2,1)}, bf16[64,64,256]{2,1,0:...) fusion(bf16[64,64,256]{2,1,0:T(8,128)(2,1)S(1)} %copy-done.3), kind=kLoop, calls=%fused_computation.46 | loop fusion | bytes 18874368 | tf_op jit(solution)/shard_map/slice | solution.py:38
  28.4 38.6 %all-to-all-done.2 = bf16[64,64,256]{2,0,1:T(8,128)(2,1)} async-done(((bf16[64,64,256]{2,0,1:T(8,128)(2,1)}), bf16[64,64,256]{2,0,1:T(8,128)(2,1)}, u32[]{:S(2)}, u32[]{:S(2)}) %all-to-all-start.2) | async-done | bytes 2097184 | tf_op jit(solution)/shard_map/all_to_all | solution.py:50
  67.0 2.9 copy.33
  69.9 0.7 fusion.38
  70.7 0.7 fusion.42
  71.4 2.1 add_convert_fusion
  73.5 4.8 %all-to-all-start.3 = ((bf16[512,8,256]{2,1,0:T(8,128)(2,1)}), bf16[512,8,256]{2,1,0:T(8,128)(2,1)}, u32[]{:S(2)}, u32[]{:S(2)}) async-start(bf16[512,8,256]{2,1,0:T(8,128)(2,1)} %bitcast.239), calls=%async_computation.3 | async-start | bytes 4194304 | tf_op jit(solution)/shard_map/all_to_all | solution.py:46
  78.3 2.4 fusion.63
  81.5 0.9 copy-done.16
  83.1 0.9 copy-done.13
  84.7 0.8 convolution_add_fusion.13
  85.5 0.8 copy-done.10
  87.0 0.9 copy-done.8
  88.6 0.9 copy-done.6
  89.4 2.7 convolution_add_fusion.10
  92.1 34.0 %all-to-all-done.3 = bf16[512,8,256]{2,1,0:T(8,128)(2,1)} async-done(((bf16[512,8,256]{2,1,0:T(8,128)(2,1)}), bf16[512,8,256]{2,1,0:T(8,128)(2,1)}, u32[]{:S(2)}, u32[]{:S(2)}) %all-to-all-start.3) | async-done | bytes 2097184 | tf_op jit(solution)/shard_map/all_to_all | solution.py:46
  126.1 2.0 convert_bitcast_fusion
  128.7 1.6 copy-done.23
  130.9 3.5 fusion.2
  134.4 2.5 copy.29
  137.0 4.9 %all-to-all-start = ((bf16[64,64,256]{2,0,1:T(8,128)(2,1)}), bf16[64,64,256]{2,0,1:T(8,128)(2,1)}, u32[]{:S(2)}, u32[]{:S(2)}) async-start(bf16[64,64,256]{2,0,1:T(8,128)(2,1)} %copy.29), calls=%async_computation | async-start | bytes 4194304 | tf_op jit(solution)/shard_map/all_to_all | solution.py:49
  141.9 3.1 fusion.35
  145.3 0.8 fusion.34
  146.1 0.8 copy-done.17
  146.9 0.8 fusion.33
  147.7 0.8 copy-done.14
  148.5 0.8 fusion.32
  149.3 1.0 fusion.31
  150.9 0.8 fusion.30
  151.7 0.8 copy-done.9
  152.5 0.8 fusion.29
  153.3 0.8 copy-done.7
  154.1 0.8 fusion.28
  154.9 0.8 copy-done.26
  155.7 0.8 fusion.27
  156.4 1.4 copy-done.24
  157.8 10.4 %pad_slice_fusion.2 = (bf16[64,64,256]{2,1,0:T(8,128)(2,1)}, bf16[64,64,256]{2,1,0:T(8,128)(2,1)S(1)}, bf16[64,64,256]{2,1,0:T(8,128)(2,1)S(1)}, bf16[64,64,256]...) fusion(bf16[64,64,256]{2,1,0:T(8,128)(2,1)S(1)} %bitcast.256), kind=kLoop, calls=%fused_computation.38 | loop fusion | bytes 18874368 | tf_op jit(solution)/shard_map/slice | solution.py:97
  168.3 0.8 convolution_add_fusion.8
  169.1 0.7 convolution_add_fusion.7
  169.8 0.7 convolution_add_fusion.6
  170.6 0.7 convolution_add_fusion.5
  171.3 2.8 convolution_add_fusion.4
  174.1 15.5 %all-to-all-done = bf16[64,64,256]{2,0,1:T(8,128)(2,1)} async-done(((bf16[64,64,256]{2,0,1:T(8,128)(2,1)}), bf16[64,64,256]{2,0,1:T(8,128)(2,1)}, u32[]{:S(2)}, u32[]{:S(2)}) %all-to-all-start) | async-done | bytes 2097184 | tf_op jit(solution)/shard_map/all_to_all | solution.py:49
  189.6 3.0 copy.30
  192.7 0.8 fusion.12
  194.4 0.7 fusion.44
  195.1 2.0 add_convert_fusion.1
  197.1 4.4 %all-to-all-start.1 = ((bf16[512,8,256]{2,1,0:T(8,128)(2,1)}), bf16[512,8,256]{2,1,0:T(8,128)(2,1)}, u32[]{:S(2)}, u32[]{:S(2)}) async-start(bf16[512,8,256]{2,1,0:T(8,128)(2,1)} %bitcast.238), calls=%async_computation.1 | async-start | bytes 4194304 | tf_op jit(solution)/shard_map/all_to_all | solution.py:46
  202.0 1.3 copy-done.2
  203.3 0.7 fusion.17
  204.1 0.7 fusion.22
  204.8 0.9 pad_maximum_fusion
  205.8 3.7 convolution_add_fusion.3
  209.5 0.8 convolution_add_fusion.2
  210.3 0.8 copy-done.15
  211.1 0.7 convolution_add_fusion.1
  211.8 0.8 copy-done.12
  212.7 2.1 fusion
  214.8 154.8 %all-reduce.7.cloned.1.call-done = (f32[3,3,256,256]{3,2,1,0:T(8,128)}, f32[3,256,256]{2,1,0:T(8,128)}) async-done(((f32[3,3,256,256]{3,2,1,0:T(8,128)}, f32[3,256,256]{2,1,0:T(8,128)}), (f32[3,3,256,256]{3,2,1,0:T(8,128)}, f32[3,256,256]{2,1,0:T(8,128)})) %all-reduce.7.cloned.1.call-update) | async-done | bytes 3145744 | tf_op jit(solution)/shard_map/psum | solution.py:103
  369.6 2.1 broadcast_multiply_fusion.1
  371.6 3.4 broadcast_multiply_fusion
  375.1 3.6 fusion.1
  (54 shorter events, 7.3 us)
Async XLA Ops:
  11.2 7.4 %copy-start.3 = (bf16[64,64,256]{2,1,0:T(8,128)(2,1)S(1)}, bf16[64,64,256]{2,1,0:T(8,128)(2,1)}, u32[]{:S(2)}) copy-start(bf16[64,64,256]{2,1,0:T(8,128)(2,1)} %param.4) | copy-start | bytes 6291460
  11.3 55.8 %all-to-all-start.2 = ((bf16[64,64,256]{2,0,1:T(8,128)(2,1)}), bf16[64,64,256]{2,0,1:T(8,128)(2,1)}, u32[]{:S(2)}, u32[]{:S(2)}) async-start(bf16[64,64,256]{2,0,1:T(8,128)(2,1)} %copy.32), calls=%async_computation.2 | async-start | bytes 4194304 | tf_op jit(solution)/shard_map/all_to_all | solution.py:50
  67.0 2.9 copy-start.27
  69.9 1.5 copy-start
  73.5 4.8 %copy-start.22 = (bf16[3,3,256,256]{3,2,1,0:T(8,128)(2,1)S(1)}, bf16[3,3,256,256]{3,2,1,0:T(8,128)(2,1)}, u32[]{:S(2)}) copy-start(bf16[3,3,256,256]{3,2,1,0:T(8,128)(2,1)} %param.5) | copy-start | bytes 3538948
  73.5 52.6 %all-to-all-start.3 = ((bf16[512,8,256]{2,1,0:T(8,128)(2,1)}), bf16[512,8,256]{2,1,0:T(8,128)(2,1)}, u32[]{:S(2)}, u32[]{:S(2)}) async-start(bf16[512,8,256]{2,1,0:T(8,128)(2,1)} %bitcast.239), calls=%async_computation.3 | async-start | bytes 4194304 | tf_op jit(solution)/shard_map/all_to_all | solution.py:46
  78.3 2.5 copy-start.19
  80.8 1.6 copy-start.16
  82.4 1.6 copy-start.13
  84.7 1.6 copy-start.10
  86.3 1.6 copy-start.8
  87.8 1.6 copy-start.6
  128.1 2.2 copy-start.23
  128.1 2.9 copy-start.25
  137.0 52.7 %all-to-all-start = ((bf16[64,64,256]{2,0,1:T(8,128)(2,1)}), bf16[64,64,256]{2,0,1:T(8,128)(2,1)}, u32[]{:S(2)}, u32[]{:S(2)}) async-start(bf16[64,64,256]{2,0,1:T(8,128)(2,1)} %copy.29), calls=%async_computation | async-start | bytes 4194304 | tf_op jit(solution)/shard_map/all_to_all | solution.py:49
  141.9 3.1 copy-start.20
  141.9 3.5 copy-start.21
  145.3 1.6 copy-start.17
  146.9 1.6 copy-start.14
  149.3 1.6 copy-start.11
  150.9 1.6 copy-start.9
  152.5 1.6 copy-start.7
  154.1 1.6 copy-start.26
  156.4 1.4 copy-start.24
  157.8 10.5 %copy-start.5 = (bf16[64,64,256]{2,1,0:T(8,128)(2,1)S(1)}, bf16[64,64,256]{2,1,0:T(8,128)(2,1)}, u32[]{:S(2)}) copy-start(bf16[64,64,256]{2,1,0:T(8,128)(2,1)} %param.7) | copy-start | bytes 6291460
  189.6 3.0 copy-start.1
  192.7 1.0 copy-start.28
  197.1 178.0 %all-to-all-start.1 = ((bf16[512,8,256]{2,1,0:T(8,128)(2,1)}), bf16[512,8,256]{2,1,0:T(8,128)(2,1)}, u32[]{:S(2)}, u32[]{:S(2)}) async-start(bf16[512,8,256]{2,1,0:T(8,128)(2,1)} %bitcast.238), calls=%async_computation.1 | async-start | bytes 4194304 | tf_op jit(solution)/shard_map/all_to_all | solution.py:46
  201.5 168.1 %all-reduce.7.cloned.1.call-start = ((), (), s32[]{:S(2)}) async-start(), calls=%async_computation.4 | async-start | bytes 6291456 | tf_op jit(solution)/shard_map/psum | solution.py:103
  201.7 1.6 copy-start.2
  205.8 3.7 copy-start.18
  209.5 1.6 copy-start.15
  211.1 1.6 copy-start.12
  371.6 3.4 copy-start.4
Sparse Core Ops, SparseCore 0:
  208.5 160.9 all-reduce.6
where the time goes:
time: 393 us; the launch traced here: 386 us
  waiting for transfers between devices  243 us (62%)
  local copies, waits for them, and re-layouts  49.7 us (13%)
  matrix products  44.8 us (11%)
  starting transfers between devices  21.7 us (6%)
  between operations  14.7 us (4%)
  other arithmetic  12 us (3%)
    psum x1, waiting for transfers between devices, local(): lax.psum((grad_spatial, grad_temporal), ('dp', 'sp'))  155 us
    all_to_all x1, waiting for transfers between devices, local(): lax.all_to_all(cotangent, 'sp', split_axis=1, concat_axis=0, tiled=True)  38.6 us
    all_to_all x2, waiting for transfers between devices, to_frames(): return lax.all_to_all(values, 'sp', split_axis=0, concat_axis=1, tiled=True)  34 us
    unnamed x59, local copies, waits for them, and re-layouts  20.2 us
    all_to_all x1, waiting for transfers between devices, local(): lax.all_to_all(act, 'sp', split_axis=1, concat_axis=0, tiled=True)  15.5 us
    dot_general x9, matrix products, times_transpose(): lax.dot_general(left, weight, (((1,), (1,)), ((), ())), preferred_element...  13.1 us
    dot_general x9, matrix products, local(): jnp.dot(window, spatial_weight[tap_row, tap_col], preferred_element_type=...  13 us
    slice x1, local copies, waits for them, and re-layouts, local(): grad_padded[2 - tap_row:2 - tap_row + slab_rows, 2 - tap_col:2 - tap_col...  10.4 us
  transfers between devices with their start and end apart: 5, of which 4 were waited for; matrix products, arithmetic and copies ran while one was open for 16% of the time, Pallas kernels for 0%

commit v1 on v0

--- a/solution.py
+++ b/solution.py
@@ -3,9 +3,18 @@
 import jax.numpy as jnp
 from jax import lax
 from jax.sharding import PartitionSpec as P
+from jax.lax import psum
 
 H = 64
 FRAMES = 4
+
+
+def open_sample(x0):
+    row_axis = "sp"
+    mesh_ax = "dp"
+    for q in (row_axis, mesh_ax):
+        x0 = psum(x0, q)
+    return x0
 
 
 def contract_rows(left, right):
@@ -100,7 +109,7 @@
             )
             grad_in = grad_in + times_transpose(back_window, spatial_weight[tap_row, tap_col])
     grad_spatial = jnp.stack(spatial_terms).reshape(3, 3, channels, channels)
-    grad_spatial, grad_temporal = lax.psum((grad_spatial, grad_temporal), ("dp", "sp"))
+    grad_spatial, grad_temporal = open_sample((grad_spatial, grad_temporal))
     grad_input = grad_in.astype(jnp.bfloat16).reshape(slab_rows, width_cells, channels)
     return (block_out, grad_input, grad_spatial * grad_scale, grad_temporal * grad_scale)
 

time: 393 us -> 453 us (1.15)
  waiting for transfers between devices: 243 us -> 297 us
  matrix products: 44.8 us -> 52.9 us
    psum x1 -> x2, waiting for transfers between devices: 155 us -> 205 us  [open_sample(): x0 = psum(x0, q)]
    dot_general x3, matrix products: 3.44 us -> 8.3 us  [local(): jnp.einsum('gfpc,cd->gfpd', earlier, temporal_weight[tap_step], preferred...]
    unnamed x59 -> x69, local copies, waits for them, and re-layouts: 20.2 us -> 19.6 us
  transfers between devices with their start and end apart: 5 -> 6, of which waited for: 4 -> 5; matrix products, arithmetic and copies ran while one was open for 16% -> 14% of each run, Pallas kernels for 0% -> 0%
where the time goes in v1:
time: 453 us; the launch traced here: 446 us
  waiting for transfers between devices  297 us (66%)
  matrix products  52.9 us (12%)
  local copies, waits for them, and re-layouts  48.7 us (11%)
  starting transfers between devices  21.9 us (5%)
  between operations  14.7 us (3%)
  other arithmetic  10.8 us (2%)
    psum x2, waiting for transfers between devices, open_sample(): x0 = psum(x0, q)  205 us
    all_to_all x1, waiting for transfers between devices, local(): lax.all_to_all(cotangent, 'sp', split_axis=1, concat_axis=0, tiled=True)  38.6 us
    all_to_all x2, waiting for transfers between devices, to_frames(): return lax.all_to_all(values, 'sp', split_axis=0, concat_axis=1, tiled=True)  34 us
    all_to_all x1, waiting for transfers between devices, local(): lax.all_to_all(act, 'sp', split_axis=1, concat_axis=0, tiled=True)  19.9 us
    unnamed x69, local copies, waits for them, and re-layouts  19.6 us
    dot_general x9, matrix products, times_transpose(): lax.dot_general(left, weight, (((1,), (1,)), ((), ())), preferred_element...  16.6 us
    dot_general x9, matrix products, local(): jnp.dot(window, spatial_weight[tap_row, tap_col], preferred_element_type=...  12.9 us
    slice x1, local copies, waits for them, and re-layouts, local(): grad_padded[2 - tap_row:2 - tap_row + slab_rows, 2 - tap_col:2 - tap_col...  9.97 us
  transfers between devices with their start and end apart: 6, of which 5 were waited for; matrix products, arithmetic and copies ran while one was open for 14% of the time, Pallas kernels for 0%

profile of v1, /device:TPU:0, one launch (start us, length us, event | category | flops | bytes accessed | tf_op | source)
XLA Modules:
  0.0 446.2 jit_solution(15040755272637693357)
XLA Ops:
  7.2 4.1 copy.32
  11.3 7.4 %all-to-all-start.2 = ((bf16[64,64,256]{2,0,1:T(8,128)(2,1)}), bf16[64,64,256]{2,0,1:T(8,128)(2,1)}, u32[]{:S(2)}, u32[]{:S(2)}) async-start(bf16[64,64,256]{2,0,1:T(8,128)(2,1)} %copy.32), calls=%async_computation.2 | async-start | bytes 4194304 | tf_op jit(solution)/shard_map/all_to_all | solution.py:59
  18.7 9.8 %pad_slice_fusion.10 = (bf16[64,64,256]{2,1,0:T(8,128)(2,1)}, bf16[64,64,256]{2,1,0:T(8,128)(2,1)}, bf16[64,64,256]{2,1,0:T(8,128)(2,1)}, bf16[64,64,256]{2,1,0:...) fusion(bf16[64,64,256]{2,1,0:T(8,128)(2,1)S(1)} %copy-done.2), kind=kLoop, calls=%fused_computation.46 | loop fusion | bytes 18874368 | tf_op jit(solution)/shard_map/slice | solution.py:47
  28.5 38.6 %all-to-all-done.2 = bf16[64,64,256]{2,0,1:T(8,128)(2,1)} async-done(((bf16[64,64,256]{2,0,1:T(8,128)(2,1)}), bf16[64,64,256]{2,0,1:T(8,128)(2,1)}, u32[]{:S(2)}, u32[]{:S(2)}) %all-to-all-start.2) | async-done | bytes 2097184 | tf_op jit(solution)/shard_map/all_to_all | solution.py:59
  67.0 2.9 copy.33
  69.9 0.7 fusion.38
  71.4 2.1 add_convert_fusion
  73.5 4.8 %all-to-all-start.3 = ((bf16[512,8,256]{2,1,0:T(8,128)(2,1)}), bf16[512,8,256]{2,1,0:T(8,128)(2,1)}, u32[]{:S(2)}, u32[]{:S(2)}) async-start(bf16[512,8,256]{2,1,0:T(8,128)(2,1)} %bitcast.239), calls=%async_computation.3 | async-start | bytes 4194304 | tf_op jit(solution)/shard_map/all_to_all | solution.py:55
  78.3 2.4 fusion.63
  81.5 0.9 copy-done.19
  83.1 0.9 copy-done.17
  84.7 0.8 convolution_add_fusion.13
  85.5 0.8 copy-done.15
  87.0 0.9 copy-done.13
  88.6 0.9 copy-done.11
  89.4 2.7 convolution_add_fusion.10
  92.1 34.0 %all-to-all-done.3 = bf16[512,8,256]{2,1,0:T(8,128)(2,1)} async-done(((bf16[512,8,256]{2,1,0:T(8,128)(2,1)}), bf16[512,8,256]{2,1,0:T(8,128)(2,1)}, u32[]{:S(2)}, u32[]{:S(2)}) %all-to-all-start.3) | async-done | bytes 2097184 | tf_op jit(solution)/shard_map/all_to_all | solution.py:55
  126.1 2.0 convert_bitcast_fusion
  128.7 1.6 copy-done.28
  130.9 3.5 fusion.2
  134.4 2.5 copy.29
  136.9 4.4 all-to-all-start
  141.9 3.1 fusion.35
  145.4 0.8 fusion.34
  146.1 0.8 copy-done.20
  147.0 0.8 fusion.33
  147.7 0.8 copy-done.18
  148.5 0.8 fusion.32
  149.3 1.0 fusion.31
  150.9 0.8 fusion.30
  151.7 0.8 copy-done.14
  152.5 0.8 fusion.29
  153.3 0.8 copy-done.12
  154.1 0.8 fusion.28
  154.9 0.8 copy-done.31
  155.7 0.8 fusion.27
  156.5 10.0 %pad_slice_fusion.2 = (bf16[64,64,256]{2,1,0:T(8,128)(2,1)}, bf16[64,64,256]{2,1,0:T(8,128)(2,1)}, bf16[64,64,256]{2,1,0:T(8,128)(2,1)}, bf16[64,64,256]{2,1,0:T...) fusion(bf16[64,64,256]{2,1,0:T(8,128)(2,1)S(1)} %bitcast.240), kind=kLoop, calls=%fused_computation.38 | loop fusion | bytes 18874368 | tf_op jit(solution)/shard_map/slice | solution.py:106
  166.4 2.7 convolution_add_fusion.8
  169.1 19.9 %all-to-all-done = bf16[64,64,256]{2,0,1:T(8,128)(2,1)} async-done(((bf16[64,64,256]{2,0,1:T(8,128)(2,1)}), bf16[64,64,256]{2,0,1:T(8,128)(2,1)}, u32[]{:S(2)}, u32[]{:S(2)}) %all-to-all-start) | async-done | bytes 2097184 | tf_op jit(solution)/shard_map/all_to_all | solution.py:58
  189.1 3.0 copy.30
  192.1 0.8 fusion.12
  192.9 3.6 fusion.40
  196.8 0.7 fusion.17
  197.5 0.7 fusion.22
  198.3 0.9 pad_maximum_fusion
  199.3 1.8 fusion.44
  201.5 2.9 add_convert_fusion.1
  204.4 4.5 %all-to-all-start.1 = ((bf16[512,8,256]{2,1,0:T(8,128)(2,1)}), bf16[512,8,256]{2,1,0:T(8,128)(2,1)}, u32[]{:S(2)}, u32[]{:S(2)}) async-start(bf16[512,8,256]{2,1,0:T(8,128)(2,1)} %bitcast.238), calls=%async_computation.1 | async-start | bytes 4194304 | tf_op jit(solution)/shard_map/all_to_all | solution.py:55
  209.2 3.1 convolution_add_fusion.7
  212.3 0.7 convolution_add_fusion.6
  213.0 0.8 copy-done.24
  213.9 0.7 convolution_add_fusion.5
  214.6 0.9 copy-done.7
  215.5 0.7 convolution_add_fusion.4
  216.3 0.8 copy-done.23
  217.1 2.7 convolution_add_fusion.3
  219.8 144.9 %all-reduce.9.cloned.1.call-done = (f32[3,3,256,256]{3,2,1,0:T(8,128)}, f32[3,256,256]{2,1,0:T(8,128)}) async-done(((f32[3,3,256,256]{3,2,1,0:T(8,128)}, f32[3,256,256]{2,1,0:T(8,128)}), (f32[3,3,256,256]{3,2,1,0:T(8,128)}, f32[3,256,256]{2,1,0:T(8,128)})) %all-reduce.9.cloned.1.call-update) | async-done | bytes 3145744 | tf_op jit(solution)/shard_map/psum | solution.py:16
  364.7 3.1 convolution_add_fusion.2
  368.5 0.8 copy-done.8
  369.4 2.1 fusion
  371.4 3.6 fusion.1
  375.1 59.8 %all-reduce.11.cloned.1.call-done = (f32[3,3,256,256]{3,2,1,0:T(8,128)}, f32[3,256,256]{2,1,0:T(8,128)}) async-done(((f32[3,3,256,256]{3,2,1,0:T(8,128)}, f32[3,256,256]{2,1,0:T(8,128)}), (f32[3,3,256,256]{3,2,1,0:T(8,128)}, f32[3,256,256]{2,1,0:T(8,128)})) %all-reduce.11.cloned.1.call-update) | async-done | bytes 3145744 | tf_op jit(solution)/shard_map/psum | solution.py:16
  434.8 3.3 broadcast_multiply_fusion
  438.2 0.9 broadcast_multiply_fusion.1
  (67 shorter events, 8.9 us)
Async XLA Ops:
  11.2 7.4 %copy-start.2 = (bf16[64,64,256]{2,1,0:T(8,128)(2,1)S(1)}, bf16[64,64,256]{2,1,0:T(8,128)(2,1)}, u32[]{:S(2)}) copy-start(bf16[64,64,256]{2,1,0:T(8,128)(2,1)} %param.4) | copy-start | bytes 6291460
  11.3 55.8 %all-to-all-start.2 = ((bf16[64,64,256]{2,0,1:T(8,128)(2,1)}), bf16[64,64,256]{2,0,1:T(8,128)(2,1)}, u32[]{:S(2)}, u32[]{:S(2)}) async-start(bf16[64,64,256]{2,0,1:T(8,128)(2,1)} %copy.32), calls=%async_computation.2 | async-start | bytes 4194304 | tf_op jit(solution)/shard_map/all_to_all | solution.py:59
  67.0 2.9 copy-start.32
  69.9 1.5 copy-start
  73.5 4.8 %copy-start.27 = (bf16[3,3,256,256]{3,2,1,0:T(8,128)(2,1)S(1)}, bf16[3,3,256,256]{3,2,1,0:T(8,128)(2,1)}, u32[]{:S(2)}) copy-start(bf16[3,3,256,256]{3,2,1,0:T(8,128)(2,1)} %param.5) | copy-start | bytes 3538948
  73.5 52.6 %all-to-all-start.3 = ((bf16[512,8,256]{2,1,0:T(8,128)(2,1)}), bf16[512,8,256]{2,1,0:T(8,128)(2,1)}, u32[]{:S(2)}, u32[]{:S(2)}) async-start(bf16[512,8,256]{2,1,0:T(8,128)(2,1)} %bitcast.239), calls=%async_computation.3 | async-start | bytes 4194304 | tf_op jit(solution)/shard_map/all_to_all | solution.py:55
  78.3 2.5 copy-start.21
  80.8 1.6 copy-start.19
  82.4 1.6 copy-start.17
  84.7 1.6 copy-start.15
  86.3 1.6 copy-start.13
  87.8 1.6 copy-start.11
  128.1 2.2 copy-start.28
  128.1 2.9 copy-start.30
  136.9 52.2 %all-to-all-start = ((bf16[64,64,256]{2,0,1:T(8,128)(2,1)}), bf16[64,64,256]{2,0,1:T(8,128)(2,1)}, u32[]{:S(2)}, u32[]{:S(2)}) async-start(bf16[64,64,256]{2,0,1:T(8,128)(2,1)} %copy.29), calls=%async_computation | async-start | bytes 4194304 | tf_op jit(solution)/shard_map/all_to_all | solution.py:58
  141.3 223.3 %all-reduce.9.cloned.1.call-start = ((), (), s32[]{:S(2)}) async-start(), calls=%async_computation.4 | async-start | bytes 6291456 | tf_op jit(solution)/shard_map/psum | solution.py:16
  141.9 3.1 copy-start.6
  141.9 3.5 copy-start.22
  145.4 1.6 copy-start.20
  147.0 1.6 copy-start.18
  149.3 1.6 copy-start.16
  150.9 1.6 copy-start.14
  152.5 1.6 copy-start.12
  154.1 1.6 copy-start.31
  156.4 10.0 %copy-start.29 = (f32[9,256,256]{2,1,0:T(8,128)}, f32[9,256,256]{2,1,0:T(8,128)S(1)}, u32[]{:S(2)}) copy-start(f32[9,256,256]{2,1,0:T(8,128)S(1)} %fusion.27) | copy-start | bytes 7077892
  156.4 10.0 %copy-start.5 = (bf16[64,64,256]{2,1,0:T(8,128)(2,1)S(1)}, bf16[64,64,256]{2,1,0:T(8,128)(2,1)}, u32[]{:S(2)}) copy-start(bf16[64,64,256]{2,1,0:T(8,128)(2,1)} %param.7) | copy-start | bytes 6291460
  189.1 3.0 copy-start.1
  199.2 2.3 copy-start.4
  204.4 4.7 %copy-start.26 = (bf16[64,64,256]{2,1,0:T(8,128)(2,1)S(1)}, bf16[64,64,256]{2,1,0:T(8,128)(2,1)}, u32[]{:S(2)}) copy-start(bf16[64,64,256]{2,1,0:T(8,128)(2,1)} %get-tuple-element.13) | copy-start | bytes 6291460
  204.4 167.0 %all-to-all-start.1 = ((bf16[512,8,256]{2,1,0:T(8,128)(2,1)}), bf16[512,8,256]{2,1,0:T(8,128)(2,1)}, u32[]{:S(2)}, u32[]{:S(2)}) async-start(bf16[512,8,256]{2,1,0:T(8,128)(2,1)} %bitcast.238), calls=%async_computation.1 | async-start | bytes 4194304 | tf_op jit(solution)/shard_map/all_to_all | solution.py:55
  208.9 225.9 %all-reduce.11.cloned.1.call-start = ((), (), s32[]{:S(2)}) async-start(), calls=%async_computation.5 | async-start | bytes 6291456 | tf_op jit(solution)/shard_map/psum | solution.py:16
  209.2 3.1 copy-start.25
  212.3 1.6 copy-start.24
  213.9 1.6 copy-start.7
  215.5 1.6 copy-start.23
  219.8 144.9 %copy-start.10 = (bf16[64,64,256]{2,1,0:T(8,128)(2,1)S(1)}, bf16[64,64,256]{2,1,0:T(8,128)(2,1)}, u32[]{:S(2)}) copy-start(bf16[64,64,256]{2,1,0:T(8,128)(2,1)} %get-tuple-element.17) | copy-start | bytes 6291460
  364.7 3.1 copy-start.9
  367.8 1.6 copy-start.8
  369.4 2.1 copy-start.3
  434.8 3.4 copy-start.33
Sparse Core Ops, SparseCore 0:
  199.4 165.2 all-reduce.8
  367.3 67.4 all-reduce.10
